TPU v7x, 32 devices: a whole 2x2x4 slice. The times are simulated.
32 devices in a mesh: owner: 8 (over z, x), rep: 4 (over y, core).
Axes of the slice: x: 2, y: 2, z: 4, core: 2. Of those that a mesh axis runs over, the one named last changes fastest.
Arguments:
- stay_rows: bfloat16 [64, 256, 1024], P('owner', 'rep'), may hold values from -40 to 40
- stay_count: int32 [64, 4], P('owner', 'rep'), may hold values from 1 to 64, as said below
- moving_rows: bfloat16 [2048, 1024], P(('owner', 'rep')), may hold values from -5 to 5
- new_list: int32 [2048], P(('owner', 'rep')), may hold values from 0 to 63, as said below
- centroids: bfloat16 [64, 128, 1024], P('owner'), may hold values from -2 to 2
- sharpness: float32 [64], P('owner'), may hold values from 0.5 to 2
Outputs:
- refreshed: bfloat16 [64, 128, 1024], P('owner')
- mass: float32 [64, 128], P('owner', 'rep')
Inputs may be any that keep to these rules, and one draw needn't show every extreme that they name: `stay_count`: slots 0 to count - 1 of a list on a replica are live; some entry equals 64. `new_list`: within the rows of one device, each list is named at most 2 times, and on every device some list is named exactly 2 times.
All inputs are finite; a program needn't handle non-finite values.
Results may differ from a plain program's by a relative error of at most 0.0032.
Values may be sent and summed in bfloat16 or wider, within the bound.
A program may use at most 64 MiB of HBM per device.

v0:
```python
import math

import jax
import jax.numpy as jnp
from jax import lax
from jax.sharding import PartitionSpec as P

SLOT_L = 2


prior_weight = 1.0


def partner(value, axis, stride):
    mask = 2**stride
    pairs = [(source, source ^ mask) for source in range(lax.axis_size(axis))]
    return lax.ppermute(value, axis, pairs)


def weigh(members, live_mask, centres, centre_norm, sharp, features):
    products = jnp.einsum("lrd,lfd->lrf", members, centres, preferred_element_type=jnp.float32)
    scores = sharp[:, None, None] * (2.0 * products - centre_norm[:, None, :]) / math.sqrt(features)
    weights = jax.nn.softmax(scores, axis=-1).astype(jnp.bfloat16) * live_mask[:, :, None]
    numerator = jnp.einsum("lrf,lrd->lfd", weights, members, preferred_element_type=jnp.float32)
    return (numerator, jnp.sum(weights.astype(jnp.float32), axis=1))


def local(stay_rows, stay_count, moving_rows, new_list, centroids, sharpness):
    owners = lax.axis_size("owner")
    replicas = lax.axis_size("rep")
    lists_here, capacity, features = stay_rows.shape
    fine_count = centroids.shape[1]
    centre_norm = jnp.sum(jnp.square(centroids.astype(jnp.float32)), axis=-1)
    outgoing_count = new_list.shape[0]
    order_index = jnp.arange(outgoing_count)
    earlier = (new_list[None, :] == new_list[:, None]) & (
        order_index[None, :] < order_index[:, None]
    )
    slot_index = jnp.sum(earlier.astype(jnp.int32), axis=1)
    local_list = new_list % lists_here
    target_owner = new_list // lists_here
    position = (local_list * owners + target_owner) * SLOT_L + slot_index
    slot_total = lists_here * owners * SLOT_L
    outgoing = (
        jnp.zeros((slot_total, features), jnp.bfloat16)
        .at[position]
        .set(moving_rows, unique_indices=True)
    )
    occupied = (
        jnp.zeros((slot_total,), jnp.bfloat16)
        .at[position]
        .set(jnp.ones((outgoing_count,), jnp.bfloat16), unique_indices=True)
    )
    arrived, present = (
        lax.all_to_all(
            outgoing.reshape(lists_here, owners, SLOT_L, features),
            "owner",
            split_axis=1,
            concat_axis=1,
            tiled=True,
        ),
        lax.all_to_all(
            occupied.reshape(lists_here, owners, SLOT_L),
            "owner",
            split_axis=1,
            concat_axis=1,
            tiled=True,
        ),
    )
    arrive_slots = owners * SLOT_L
    arrivals = arrived.reshape(lists_here, arrive_slots, features)
    present = present.reshape(lists_here, arrive_slots)
    live_count = stay_count[:, 0]
    replica = lax.axis_index("rep")
    fine_share = fine_count // replicas
    groups = max(1, replicas // lists_here)
    per_rep = max(1, lists_here // replicas)
    slot_mask = (jnp.arange(capacity)[None, :] < live_count[:, None]).astype(jnp.bfloat16)
    stay_pieces = stay_rows.reshape(lists_here * groups, capacity // groups, features)
    mask_pieces = slot_mask.reshape(lists_here * groups, capacity // groups)
    moved_stay, moved_mask = (
        lax.all_to_all(stay_pieces, "rep", split_axis=0, concat_axis=1, tiled=True),
        lax.all_to_all(mask_pieces, "rep", split_axis=0, concat_axis=1, tiled=True),
    )
    arrive_pieces = arrivals.reshape(lists_here * groups, arrive_slots // groups, features)
    present_pieces = present.reshape(lists_here * groups, arrive_slots // groups)
    moved_arrive, moved_present = (
        lax.all_to_all(arrive_pieces, "rep", split_axis=0, concat_axis=1, tiled=True),
        lax.all_to_all(present_pieces, "rep", split_axis=0, concat_axis=1, tiled=True),
    )
    members = jnp.concatenate([moved_stay, moved_arrive], axis=1)
    member_mask = jnp.concatenate([moved_mask, moved_present], axis=1)
    first_list = replica * per_rep // groups
    centres = lax.dynamic_slice_in_dim(centroids, first_list, per_rep, 0)
    norms = lax.dynamic_slice_in_dim(centre_norm, first_list, per_rep, 0)
    sharp = lax.dynamic_slice_in_dim(sharpness, first_list, per_rep, 0)
    numerator, mass_sum = weigh(members, member_mask, centres, norms, sharp, features)
    for bit_number in range(groups.bit_length() - 1):
        other_num, other_mass = partner((numerator, mass_sum), "rep", bit_number)
        numerator = numerator + other_num
        mass_sum = mass_sum + other_mass
    refreshed_all = (
        (numerator + prior_weight * centres.astype(jnp.float32))
        / (mass_sum[:, :, None] + prior_weight)
    ).astype(jnp.bfloat16)
    piece_rows = fine_count // groups
    part_index = replica % groups
    refreshed_piece = lax.dynamic_slice_in_dim(
        refreshed_all, part_index * piece_rows, piece_rows, 1
    ).reshape(per_rep * piece_rows, features)
    mass_piece = lax.dynamic_slice_in_dim(mass_sum, part_index * piece_rows, piece_rows, 1).reshape(
        per_rep * piece_rows
    )
    refreshed = lax.all_gather(refreshed_piece, "rep", axis=0, tiled=True).reshape(
        lists_here, fine_count, features
    )
    mass_whole = lax.all_gather(mass_piece, "rep", axis=0, tiled=True).reshape(
        lists_here, fine_count
    )
    return (refreshed, lax.dynamic_slice_in_dim(mass_whole, replica * fine_share, fine_share, 1))


def solution(mesh):
    in_specs = (
        P("owner", "rep", None),
        P("owner", "rep"),
        P(("owner", "rep"), None),
        P(("owner", "rep")),
        P("owner", None, None),
        P("owner"),
    )
    out_specs = (P("owner", None, None), P("owner", "rep"))
    return jax.shard_map(local, mesh=mesh, in_specs=in_specs, out_specs=out_specs, check_vma=False)
```

profile of v0, /device:TPU:0, one launch (start us, length us, event | category | flops | bytes accessed | tf_op | source)
XLA Modules:
  0.0 113.6 jit_solution(16285201759303111877)
XLA Ops:
  7.2 0.9 convert_reduce_fusion.1
  8.1 0.7 compare_select_fusion
  8.8 1.0 scatter_custom_fusion.1
  9.7 0.1 reshape.54
  9.9 0.1 copy.37
  10.0 13.5 %all_to_all.81 = bf16[8,8,2]{0,2,1:T(2,128)(2,1)S(1)} all-to-all(bf16[8,8,2]{0,2,1:T(2,128)(2,1)S(1)} %copy.37), channel_id=1, replica_groups=mesh['owner'=8,'rep'=4] {'owner'}, dimensions={1} | all-to-all | bytes 512 | tf_op jit(solution)/shard_map/all_to_all | solution.py:62
  23.6 0.7 copy.40
  24.3 3.2 %all-to-all-start.5 = ((bf16[4,2,16]{2,1,0:T(2,128)(2,1)}), bf16[4,2,16]{2,1,0:T(2,128)(2,1)S(1)}, u32[]{:S(2)}, u32[]{:S(2)}) async-start(bf16[4,2,16]{2,1,0:T(2,128)(2,1)} %copy.40), calls=%async_computation.5 | async-start | bytes 4096 | tf_op jit(solution)/shard_map/all_to_all | solution.py:89
  27.5 1.3 %scatter_custom_fusion = bf16[128,1024]{1,0:T(8,128)(2,1)S(1)} fusion(s32[64]{0:T(128)S(1)} %compare_select_fusion, bf16[64,1024]{1,0:T(8,128)(2,1)} %param.8, bf16[]{:T(256)} %constant.65.clone.1), kind=kCustom, calls=%fused_computation.18 | custom fusion | bytes 262656 | tf_op jit(solution)/shard_map/scatter | solution.py:47
  29.0 0.9 copy.33
  29.9 1.3 %all-to-all-done.5 = bf16[4,2,16]{2,1,0:T(2,128)(2,1)S(1)} async-done(((bf16[4,2,16]{2,1,0:T(2,128)(2,1)}), bf16[4,2,16]{2,1,0:T(2,128)(2,1)S(1)}, u32[]{:S(2)}, u32[]{:S(2)}) %all-to-all-start.5) | async-done | bytes 288 | tf_op jit(solution)/shard_map/all_to_all | solution.py:89
  31.2 3.4 %all-to-all-start.1 = ((bf16[8,8,2,1024]{3,2,0,1:T(2,128)(2,1)}), bf16[8,8,2,1024]{3,2,0,1:T(2,128)(2,1)S(1)}, u32[]{:S(2)}, u32[]{:S(2)}) async-start(bf16[8,8,2,1024]{3,2,0,1:T(2,128)(2,1)} %copy.33), calls=%async_computation.1 | async-start | bytes 524288 | tf_op jit(solution)/shard_map/all_to_all | solution.py:55
  34.6 0.5 broadcast.47
  35.1 1.3 %reduce.3 = s32[8]{0:T(128)S(1)} reduce(s32[8,1]{0,1:T(1,128)} %param.7, s32[]{:T(128)} %broadcast.47), dimensions={1}, to_apply=%param.7.reduce_sub_computation.3 | reduce | bytes 68 | tf_op args[1]
  36.5 0.7 compare_convert_fusion
  37.2 6.7 %all-to-all-done.1 = bf16[8,8,2,1024]{3,2,0,1:T(2,128)(2,1)S(1)} async-done(((bf16[8,8,2,1024]{3,2,0,1:T(2,128)(2,1)}), bf16[8,8,2,1024]{3,2,0,1:T(2,128)(2,1)S(1)}, u32[]{:S(2)}, u32[]{:S(2)}) %all-to-all-start.1) | async-done | bytes 262176 | tf_op jit(solution)/shard_map/all_to_all | solution.py:55
  43.8 3.2 %all-to-all-start.3 = ((bf16[4,2,64]{2,1,0:T(2,128)(2,1)}), bf16[4,2,64]{2,1,0:T(2,128)(2,1)S(1)}, u32[]{:S(2)}, u32[]{:S(2)}) async-start(bf16[4,2,64]{2,1,0:T(2,128)(2,1)} %compare_convert_fusion), calls=%async_computation.3 | async-start | bytes 4096 | tf_op jit(solution)/shard_map/all_to_all | solution.py:83
  47.1 0.2 copy.34
  47.4 3.3 %all-to-all-done.3 = bf16[4,2,64]{2,1,0:T(2,128)(2,1)S(1)} async-done(((bf16[4,2,64]{2,1,0:T(2,128)(2,1)}), bf16[4,2,64]{2,1,0:T(2,128)(2,1)S(1)}, u32[]{:S(2)}, u32[]{:S(2)}) %all-to-all-start.3) | async-done | bytes 1056 | tf_op jit(solution)/shard_map/all_to_all | solution.py:83
  50.7 8.4 %all_to_all.82 = bf16[8,16,1024]{2,1,0:T(8,128)(2,1)S(1)} all-to-all(bf16[8,16,1024]{2,1,0:T(8,128)(2,1)S(1)} %reshape.53), channel_id=1, replica_groups=mesh['owner'=8,'rep'=4] {'rep'}, dimensions={0} | all-to-all | bytes 524288 | tf_op jit(solution)/shard_map/all_to_all | solution.py:88
  59.1 3.5 %all-to-all-start = ((bf16[8,64,1024]{2,1,0:T(8,128)(2,1)}), bf16[8,64,1024]{2,1,0:T(8,128)(2,1)S(1)}, u32[]{:S(2)}, u32[]{:S(2)}) async-start(bf16[8,64,1024]{2,1,0:T(8,128)(2,1)} %param.6), calls=%async_computation | async-start | bytes 2097152 | tf_op jit(solution)/shard_map/all_to_all | solution.py:82
  62.8 0.5 multiply_reduce_fusion
  63.5 0.7 copy.35
  64.2 12.9 %all-to-all-done = bf16[8,64,1024]{2,1,0:T(8,128)(2,1)S(1)} async-done(((bf16[8,64,1024]{2,1,0:T(8,128)(2,1)}), bf16[8,64,1024]{2,1,0:T(8,128)(2,1)S(1)}, u32[]{:S(2)}, u32[]{:S(2)}) %all-to-all-start) | async-done | bytes 1048608 | tf_op jit(solution)/shard_map/all_to_all | solution.py:82
  77.1 1.1 copy.32
  78.2 2.1 %fusion.32 = (f32[2,320]{1,0:T(2,128)S(1)}, f32[2,320,128]{2,1,0:T(8,128)S(1)}) fusion(bf16[2,64,1024]{2,1,0:T(8,128)(2,1)} %bitcast.26, bf16[2,256,1024]{2,1,0:T(8,128)(2,1)} %bitcast.22, bf16[8,128,1024]{2,1,0:T(8,128)(2,1)S(1)} %copy-done, s32[]{:T(128)S(6)} %select_n.32, f32[2,128]{1,0:T(2,128)S(1)} %constant_dynamic-slice_fusion.1, f32[2]{0:T(128)S(1)} %dynamic_slice.14), kind=kOutput, calls=%fused_computation.46 | convolution fusion | flops 170885248 | bytes 2166788 | tf_op jit(solution)/shard_map/sub | solution.py:23
  80.3 0.3 convert_reduce_fusion
  80.6 2.3 %fusion.2 = bf16[2,128,1024]{2,1,0:T(8,128)(2,1)} fusion(bf16[2,320,128]{2,1,0:T(8,128)(2,1)S(1)} %get-tuple-element.3, bf16[2,64,1024]{2,1,0:T(8,128)(2,1)} %bitcast.27, bf16[2,256,1024]{2,1,0:T(8,128)(2,1)S(1)} %bitcast.23, f32[2,128]{1,0:T(2,128)S(1)} %broadcast_add_fusion, bf16[8,128,1024]{2,1,0:T(8,128)(2,1)S(1)} %copy-done, s32[]{:T(128)S(6)} %select_n.32), kind=kOutput, calls=%fused_computation.7 | convolution fusion | flops 171442176 | bytes 2524164 | tf_op jit(solution)/shard_map/lrf,lrd->lfd/dot_general | solution.py:24
  82.9 5.1 %all-gather = f32[4,1,256]{2,1,0:T(1,128)S(1)} all-gather(f32[1,1,256]{2,1,0:T(1,128)S(1)} %bitcast.29), channel_id=1, replica_groups=mesh['owner'=8,'rep'=4] {'rep'}, dimensions={0}, use_global_device_ids=true | all-gather | bytes 5120 | tf_op jit(solution)/shard_map/all_gather | solution.py:117
  87.9 0.7 constant_dynamic-slice_fusion
  88.6 15.1 %all-gather.3.cloned.1.call-done = bf16[1024,1024]{1,0:T(8,128)(2,1)} async-done(((bf16[256,1024]{1,0:T(8,128)(2,1)}), bf16[1024,1024]{1,0:T(8,128)(2,1)}) %all-gather.3.cloned.1.call-update) | async-done | bytes 2097168 | tf_op jit(solution)/shard_map/all_gather | solution.py:114
  103.6 3.1 %copy.42 = bf16[8,128,1024]{2,1,0:T(8,128)(2,1)} copy(bf16[8,128,1024]{2,1,0:T(8,128)(2,1)} %bitcast.21) | data formatting | bytes 4194304
  (21 shorter events, 0.7 us)
Async XLA Ops:
  24.3 6.9 %all-to-all-start.5 = ((bf16[4,2,16]{2,1,0:T(2,128)(2,1)}), bf16[4,2,16]{2,1,0:T(2,128)(2,1)S(1)}, u32[]{:S(2)}, u32[]{:S(2)}) async-start(bf16[4,2,16]{2,1,0:T(2,128)(2,1)} %copy.40), calls=%async_computation.5 | async-start | bytes 4096 | tf_op jit(solution)/shard_map/all_to_all | solution.py:89
  29.9 32.8 %copy-start.2 = (f32[8]{0:T(128)S(1)}, f32[8]{0:T(128)}, u32[]{:S(2)}) copy-start(f32[8]{0:T(128)} %param.11) | copy-start | bytes 100
  29.9 32.9 %copy-start = (bf16[8,128,1024]{2,1,0:T(8,128)(2,1)S(1)}, bf16[8,128,1024]{2,1,0:T(8,128)(2,1)}, u32[]{:S(2)}) copy-start(bf16[8,128,1024]{2,1,0:T(8,128)(2,1)} %param.10) | copy-start | bytes 6291460
  31.2 12.7 %all-to-all-start.1 = ((bf16[8,8,2,1024]{3,2,0,1:T(2,128)(2,1)}), bf16[8,8,2,1024]{3,2,0,1:T(2,128)(2,1)S(1)}, u32[]{:S(2)}, u32[]{:S(2)}) async-start(bf16[8,8,2,1024]{3,2,0,1:T(2,128)(2,1)} %copy.33), calls=%async_computation.1 | async-start | bytes 524288 | tf_op jit(solution)/shard_map/all_to_all | solution.py:55
  43.8 6.9 %all-to-all-start.3 = ((bf16[4,2,64]{2,1,0:T(2,128)(2,1)}), bf16[4,2,64]{2,1,0:T(2,128)(2,1)S(1)}, u32[]{:S(2)}, u32[]{:S(2)}) async-start(bf16[4,2,64]{2,1,0:T(2,128)(2,1)} %compare_convert_fusion), calls=%async_computation.3 | async-start | bytes 4096 | tf_op jit(solution)/shard_map/all_to_all | solution.py:83
  59.1 18.0 %all-to-all-start = ((bf16[8,64,1024]{2,1,0:T(8,128)(2,1)}), bf16[8,64,1024]{2,1,0:T(8,128)(2,1)S(1)}, u32[]{:S(2)}, u32[]{:S(2)}) async-start(bf16[8,64,1024]{2,1,0:T(8,128)(2,1)} %param.6), calls=%async_computation | async-start | bytes 2097152 | tf_op jit(solution)/shard_map/all_to_all | solution.py:82
  62.7 41.0 %all-gather.3.cloned.1.call-start = ((), (), s32[]{:S(2)}) async-start(), calls=%async_computation.6 | async-start | bytes 2621440 | tf_op jit(solution)/shard_map/all_gather | solution.py:114
  78.2 2.4 %copy-start.1 = (bf16[4,2,64,1024]{3,2,0,1:T(8,128)(2,1)S(1)}, bf16[4,2,64,1024]{3,2,0,1:T(8,128)(2,1)}, u32[]{:S(2)}) copy-start(bf16[4,2,64,1024]{3,2,0,1:T(8,128)(2,1)} %copy.32) | copy-start | bytes 3145732
Sparse Core Ops, SparseCore 0:
  83.0 20.6 all-gather.2
where the time goes:
time: 114 us
  waiting for transfers between devices  39.2 us (34%)
  blocking collectives  27 us (24%)
  between operations  14.2 us (12%)
  starting transfers between devices  13.4 us (12%)
  local copies, waits for them, and re-layouts  11.1 us (10%)
  matrix products  4.37 us (4%)
  other arithmetic  4.3 us (4%)
    all_gather x1, waiting for transfers between devices, local(): lax.all_gather(refreshed_piece, 'rep', axis=0, tiled=True)  15.1 us
    all_to_all x1, blocking collectives, local(): lax.all_to_all(occupied.reshape(lists_here, owners, SLOT_L), 'owner', spl...  13.5 us
    all_to_all x1, waiting for transfers between devices, local(): lax.all_to_all(stay_pieces, 'rep', split_axis=0, concat_axis=1, tiled=True)  12.9 us
    all_to_all x1, blocking collectives, local(): lax.all_to_all(arrive_pieces, 'rep', split_axis=0, concat_axis=1, tiled=T...  8.41 us
    all_to_all x1, waiting for transfers between devices, local(): lax.all_to_all(outgoing.reshape(lists_here, owners, SLOT_L, features), 'o...  6.67 us
    all_gather x1, blocking collectives, local(): lax.all_gather(mass_piece, 'rep', axis=0, tiled=True)  5.07 us
    unnamed x8, local copies, waits for them, and re-layouts  3.6 us
    all_to_all x1, starting transfers between devices, local(): lax.all_to_all(stay_pieces, 'rep', split_axis=0, concat_axis=1, tiled=True)  3.52 us
  transfers between devices with their start and end apart: 5, of which 5 were waited for; matrix products, arithmetic and copies ran while one was open for 6% of the time, Pallas kernels for 0%

commit v1 on v0

--- a/solution.py
+++ b/solution.py
@@ -3,6 +3,8 @@
 import jax
 import jax.numpy as jnp
 from jax import lax
+from jax.experimental import pallas as pl
+from jax.experimental.pallas import tpu as pltpu
 from jax.sharding import PartitionSpec as P
 
 SLOT_L = 2
@@ -120,6 +122,335 @@
     return (refreshed, lax.dynamic_slice_in_dim(mass_whole, replica * fine_share, fine_share, 1))
 
 
+LANES = 128
+VMEM_BUDGET = 40 * 2**20
+MESH = pl.DeviceIdType.MESH
+
+
+class Plan:
+    def __init__(self, owners, replicas, lists, capacity, features, fine, moving):
+        self.owners, self.replicas, self.lists = owners, replicas, lists
+        self.capacity, self.features, self.fine, self.moving = capacity, features, fine, moving
+        self.split = 2 if replicas % 2 == 0 and lists % 2 == 0 else 1
+        self.groups = replicas // self.split
+        self.half = lists // self.split
+        self.per_source = self.half * SLOT_L
+        self.block = self.groups * self.per_source
+        self.blocks = owners * self.split
+        self.width = features + LANES
+        self.moving_lanes = -(-moving // LANES) * LANES
+
+    def fits(self):
+        slots = 2 * self.blocks * self.block * self.width
+        held = self.half * self.replicas * self.capacity * self.features
+        centres = 2 * self.half * self.fine * self.features
+        gathered = self.groups * self.moving * self.features
+        small = 2 * (slots + held + centres + gathered)
+        return (
+            small <= VMEM_BUDGET
+            and self.block % 16 == 0
+            and self.capacity % 16 == 0
+            and self.moving % 16 == 0
+            and self.features % LANES == 0
+            and self.fine % LANES == 0
+        )
+
+
+def weigh_rows(plan, centres, norm, sharp, rows, mask):
+    products = lax.dot_general(
+        centres, rows, (((1,), (1,)), ((), ())), preferred_element_type=jnp.float32
+    )
+    scores = sharp * (2.0 * products - norm) / math.sqrt(plan.features)
+    top = jnp.max(scores, axis=0, keepdims=True)
+    raised = jnp.exp(scores - top)
+    weights = (raised / jnp.sum(raised, axis=0, keepdims=True)).astype(jnp.bfloat16)
+    weights = weights * mask.astype(jnp.bfloat16)
+    numerator = jnp.dot(weights, rows, preferred_element_type=jnp.float32)
+    mass = jnp.sum(weights.astype(jnp.float32), axis=1, keepdims=True)
+    ones = jnp.ones((8, rows.shape[0]), jnp.bfloat16)
+    mass_row = lax.dot_general(
+        ones, weights, (((1,), (1,)), ((), ())), preferred_element_type=jnp.float32
+    )
+    return numerator, mass, mass_row
+
+
+def fused_kernel(
+    plan,
+    stay_ref, count_ref, moving_ref, list_ref, centre_ref, sharp_ref,
+    out_ref, mass_ref,
+    stay_buf, count_buf, moving_buf, pos_own, pos_buf, placed, arrived, centre_buf, result_buf, mass_buf,
+    stay_send, stay_recv, count_send, count_recv, moving_send, moving_recv, pos_send, pos_recv,
+    slot_send, slot_recv, centre_sem, result_send, result_recv, mass_send, mass_recv, local_sem,
+):
+    owners, split, groups, half = plan.owners, plan.split, plan.groups, plan.half
+    replicas, capacity, features = plan.replicas, plan.capacity, plan.features
+    owner = lax.axis_index("owner")
+    replica = lax.axis_index("rep")
+    core = replica % split
+    group = replica // split
+
+    def rep_at(k, dc):
+        return lax.rem(group + k, groups) * split + lax.rem(core + dc, split)
+
+    def owner_at(k):
+        return lax.rem(owner + k, owners)
+
+    peers = [(k, dc) for k in range(groups) for dc in range(split) if (k, dc) != (0, 0)]
+    plane = [(k, dc) for k in range(1, owners) for dc in range(split)]
+    barrier = pltpu.get_barrier_semaphore()
+    for k, dc in peers:
+        pl.semaphore_signal(barrier, inc=1, device_id=(owner, rep_at(k, dc)), device_id_type=MESH)
+    for k, dc in plane:
+        pl.semaphore_signal(
+            barrier, inc=1, device_id=(owner_at(k), rep_at(0, dc)), device_id_type=MESH
+        )
+
+    centre_copy = pltpu.make_async_copy(
+        centre_ref.at[pl.ds(core * half, half)], centre_buf, centre_sem
+    )
+    centre_copy.start()
+
+    def own_copy(j):
+        return pltpu.make_async_copy(
+            stay_ref.at[core * half + j], stay_buf.at[j, 0], stay_recv.at[j, 0]
+        )
+
+    for j in range(half):
+        own_copy(j).start()
+
+    moving = plan.moving
+    count_buf[0] = jnp.broadcast_to(count_ref[...], count_buf.shape[1:])
+    names = jnp.broadcast_to(list_ref[...], (moving, moving))
+    row = lax.broadcasted_iota(jnp.int32, (moving, moving), 0)
+    column = lax.broadcasted_iota(jnp.int32, (moving, moving), 1)
+    down = jnp.sum(jnp.where(row == column, names, 0), axis=1, keepdims=True)
+    earlier = jnp.where((names == down) & (row < column), 1, 0)
+    slot = jnp.sum(earlier, axis=0, keepdims=True)
+    target = list_ref[...]
+    position = (
+        (target // half) * plan.block + group * plan.per_source + (target % half) * SLOT_L + slot
+    )
+    pos_own[...] = jnp.full(pos_own.shape, -1, jnp.int32)
+    pos_own[:, :moving] = jnp.broadcast_to(position, (8, moving))
+
+    pl.semaphore_wait(barrier, len(peers) + len(plane))
+
+    def moving_copy(k):
+        return pltpu.make_async_remote_copy(
+            src_ref=moving_ref, dst_ref=moving_buf.at[k - 1],
+            send_sem=moving_send.at[k - 1], recv_sem=moving_recv.at[k - 1],
+            device_id=(owner, rep_at(k, 0)), device_id_type=MESH,
+        )
+
+    def pos_copy(k):
+        return pltpu.make_async_remote_copy(
+            src_ref=pos_own, dst_ref=pos_buf.at[k - 1],
+            send_sem=pos_send.at[k - 1], recv_sem=pos_recv.at[k - 1],
+            device_id=(owner, rep_at(k, 0)), device_id_type=MESH,
+        )
+
+    for k in range(1, groups):
+        pos_copy(k).start()
+        moving_copy(k).start()
+
+    def count_copy(k, dc):
+        q = k * split + dc
+        return pltpu.make_async_remote_copy(
+            src_ref=count_buf.at[0], dst_ref=count_buf.at[q],
+            send_sem=count_send.at[q], recv_sem=count_recv.at[q],
+            device_id=(owner, rep_at(k, dc)), device_id_type=MESH,
+        )
+
+    def stay_copy(j, k, dc):
+        q = k * split + dc
+        return pltpu.make_async_remote_copy(
+            src_ref=stay_ref.at[lax.rem(core + dc, split) * half + j], dst_ref=stay_buf.at[j, q],
+            send_sem=stay_send.at[j, q], recv_sem=stay_recv.at[j, q],
+            device_id=(owner, rep_at(k, dc)), device_id_type=MESH,
+        )
+
+    for k, dc in peers:
+        count_copy(k, dc).start()
+    for j in range(half):
+        for k, dc in peers:
+            stay_copy(j, k, dc).start()
+
+    total = plan.blocks * plan.block
+    slot_row = lax.broadcasted_iota(jnp.int32, (total, moving), 0)
+
+    def one_hot(positions):
+        return jnp.where(slot_row == positions, 1.0, 0.0).astype(jnp.bfloat16)
+
+    pick = one_hot(pos_own[0:1, :moving])
+    ones = jnp.ones((moving, LANES), jnp.bfloat16)
+    rows = jnp.dot(pick, moving_ref[...], preferred_element_type=jnp.float32)
+    flags = jnp.dot(pick, ones, preferred_element_type=jnp.float32)
+    for k in range(1, groups):
+        pos_copy(k).wait_recv()
+        moving_copy(k).wait_recv()
+        pick = one_hot(pos_buf[k - 1, 0:1, :moving])
+        rows += jnp.dot(pick, moving_buf[k - 1], preferred_element_type=jnp.float32)
+        flags += jnp.dot(pick, ones, preferred_element_type=jnp.float32)
+    placed[:, :, :features] = rows.astype(jnp.bfloat16).reshape(plan.blocks, plan.block, features)
+    placed[:, :, features:] = flags.astype(jnp.bfloat16).reshape(plan.blocks, plan.block, LANES)
+
+    def slot_copy(k, dc):
+        b = k * split + dc
+        return pltpu.make_async_remote_copy(
+            src_ref=placed.at[owner_at(k) * split + lax.rem(core + dc, split)],
+            dst_ref=arrived.at[b],
+            send_sem=slot_send.at[b], recv_sem=slot_recv.at[b],
+            device_id=(owner_at(k), rep_at(0, dc)), device_id_type=MESH,
+        )
+
+    sent = [(k, dc) for k in range(owners) for dc in range(split) if (k, dc) != (0, 0)]
+    for k, dc in sent:
+        slot_copy(k, dc).start()
+    arrived[0] = placed[owner * split + core]
+    centre_copy.wait()
+    for k, dc in peers:
+        count_copy(k, dc).wait_recv()
+    for k, dc in sent:
+        slot_copy(k, dc).wait_recv()
+
+    lane = lax.broadcasted_iota(jnp.int32, (1, replicas * capacity), 1)
+    arrived_lane = lax.broadcasted_iota(jnp.int32, (1, total), 1)
+    arrived_list = (arrived_lane % plan.per_source) // SLOT_L
+
+    def result_copy(j, dc):
+        return pltpu.make_async_remote_copy(
+            src_ref=result_buf.at[j], dst_ref=out_ref.at[core * half + j],
+            send_sem=result_send.at[j, dc], recv_sem=result_recv.at[j, dc],
+            device_id=(owner, rep_at(0, dc)), device_id_type=MESH,
+        )
+
+    def result_own(j):
+        return pltpu.make_async_copy(
+            result_buf.at[j], out_ref.at[core * half + j], result_recv.at[j, 0]
+        )
+
+    def one_list(j, carry):
+        own_copy(j).wait()
+        for k, dc in peers:
+            stay_copy(j, k, dc).wait_recv()
+        centres = centre_buf[j]
+        wide = centres.astype(jnp.float32)
+        norm = jnp.sum(wide * wide, axis=1, keepdims=True)
+        sharp = sharp_ref[core * half + j]
+        counts = count_buf[0, pl.ds(core * half + j, 1), :]
+        for q in range(1, replicas):
+            counts = jnp.where(
+                lane // capacity == q, count_buf[q, pl.ds(core * half + j, 1), :], counts
+            )
+        mask = jnp.where(lane % capacity < counts, 1.0, 0.0)
+        members = stay_buf[j].reshape(replicas * capacity, features)
+        num, mass, mass_row = weigh_rows(plan, centres, norm, sharp, members, mask)
+        rows = arrived[:, :, :features].reshape(total, features)
+        marks = arrived[:, :, features:].reshape(total, LANES)
+        spread = jnp.full((8, LANES), 1.0 / LANES, jnp.bfloat16)
+        present = lax.dot_general(
+            spread, marks, (((1,), (1,)), ((), ())), preferred_element_type=jnp.float32
+        )[0:1]
+        here = jnp.where(arrived_list == j, present, 0.0)
+        num2, mass2, mass_row2 = weigh_rows(plan, centres, norm, sharp, rows, here)
+        mass = mass + mass2
+        result_buf[j] = (
+            (num + num2 + prior_weight * wide) / (mass + prior_weight)
+        ).astype(jnp.bfloat16)
+        mass_buf[j] = mass_row + mass_row2
+        result_own(j).start()
+        for dc in range(1, split):
+            result_copy(j, dc).start()
+        return carry
+
+    lax.fori_loop(0, half, one_list, 0)
+
+    def mass_copy(dc):
+        return pltpu.make_async_remote_copy(
+            src_ref=mass_buf, dst_ref=mass_ref.at[core],
+            send_sem=mass_send.at[dc], recv_sem=mass_recv.at[dc],
+            device_id=(owner, rep_at(0, dc)), device_id_type=MESH,
+        )
+
+    mass_own = pltpu.make_async_copy(mass_buf, mass_ref.at[core], local_sem)
+    mass_own.start()
+    for dc in range(1, split):
+        mass_copy(dc).start()
+
+    for k in range(1, groups):
+        pos_copy(k).wait_send()
+        moving_copy(k).wait_send()
+    for k, dc in peers:
+        count_copy(k, dc).wait_send()
+    for j in range(half):
+        for k, dc in peers:
+            stay_copy(j, k, dc).wait_send()
+    for k, dc in sent:
+        slot_copy(k, dc).wait_send()
+    for j in range(half):
+        result_own(j).wait()
+        for dc in range(1, split):
+            result_copy(j, dc).wait()
+    mass_own.wait()
+    for dc in range(1, split):
+        mass_copy(dc).wait()
+
+
+def fused(plan, stay_rows, stay_count, moving_rows, new_list, centroids, sharpness):
+    half, split, replicas = plan.half, plan.split, plan.replicas
+    any_space = pl.BlockSpec(memory_space=pl.ANY)
+    vmem = pl.BlockSpec(memory_space=pltpu.VMEM)
+    dma = pltpu.SemaphoreType.DMA
+    members = replicas * plan.capacity
+    refreshed, mass = pl.pallas_call(
+        lambda *refs: fused_kernel(plan, *refs),
+        out_shape=(
+            jax.ShapeDtypeStruct(centroids.shape, jnp.bfloat16),
+            jax.ShapeDtypeStruct((split, half, 8, plan.fine), jnp.float32),
+        ),
+        in_specs=[any_space, vmem, vmem, vmem, any_space, pl.BlockSpec(memory_space=pltpu.SMEM)],
+        out_specs=(any_space, any_space),
+        scratch_shapes=[
+            pltpu.VMEM((half, replicas, plan.capacity, plan.features), jnp.bfloat16),
+            pltpu.VMEM((replicas, plan.lists, members), jnp.int32),
+            pltpu.VMEM((max(1, plan.groups - 1), plan.moving, plan.features), jnp.bfloat16),
+            pltpu.VMEM((8, plan.moving_lanes), jnp.int32),
+            pltpu.VMEM((max(1, plan.groups - 1), 8, plan.moving_lanes), jnp.int32),
+            pltpu.VMEM((plan.blocks, plan.block, plan.width), jnp.bfloat16),
+            pltpu.VMEM((plan.blocks, plan.block, plan.width), jnp.bfloat16),
+            pltpu.VMEM((half, plan.fine, plan.features), jnp.bfloat16),
+            pltpu.VMEM((half, plan.fine, plan.features), jnp.bfloat16),
+            pltpu.VMEM((half, 8, plan.fine), jnp.float32),
+            dma((half, replicas)), dma((half, replicas)),
+            dma((replicas,)), dma((replicas,)),
+            dma((plan.groups,)), dma((plan.groups,)),
+            dma((plan.groups,)), dma((plan.groups,)),
+            dma((plan.blocks,)), dma((plan.blocks,)),
+            dma,
+            dma((half, split)), dma((half, split)),
+            dma((split,)), dma((split,)),
+            dma,
+        ],
+        compiler_params=pltpu.CompilerParams(
+            collective_id=0, has_side_effects=True, vmem_limit_bytes=48 * 2**20
+        ),
+    )(stay_rows, stay_count, moving_rows, new_list.reshape(1, -1), centroids, sharpness)
+    fine_share = plan.fine // replicas
+    whole = mass[:, :, 0, :].reshape(plan.lists, plan.fine)
+    share = lax.dynamic_slice_in_dim(whole, lax.axis_index("rep") * fine_share, fine_share, 1)
+    return refreshed, share
+
+
+def device_program(stay_rows, stay_count, moving_rows, new_list, centroids, sharpness):
+    lists_here, capacity, features = stay_rows.shape
+    plan = Plan(
+        lax.axis_size("owner"), lax.axis_size("rep"), lists_here, capacity, features,
+        centroids.shape[1], moving_rows.shape[0],
+    )
+    step = (lambda *a: fused(plan, *a)) if plan.fits() else local
+    return step(stay_rows, stay_count, moving_rows, new_list, centroids, sharpness)
+
+
 def solution(mesh):
     in_specs = (
         P("owner", "rep", None),
@@ -130,4 +461,4 @@
         P("owner"),
     )
     out_specs = (P("owner", None, None), P("owner", "rep"))
-    return jax.shard_map(local, mesh=mesh, in_specs=in_specs, out_specs=out_specs, check_vma=False)
+    return jax.shard_map(device_program, mesh=mesh, in_specs=in_specs, out_specs=out_specs, check_vma=False)

time: 114 us -> 46.1 us (0.40)
  waiting for transfers between devices: 39.2 us -> 0 us
  Pallas kernels: 0 us -> 37.5 us
  blocking collectives: 27 us -> 0 us
  between operations: 14.2 us -> 0.66 us
  starting transfers between devices: 13.4 us -> 0 us
  matrix products: 4.37 us -> 0 us
  other arithmetic: 4.3 us -> 0 us
  local copies, waits for them, and re-layouts: 11.1 us -> 7.75 us
    pallas_call x0 -> x1, Pallas kernels: none -> 37.5 us  [fused(): pl.pallas_call(lambda *refs: fused_kernel(plan, *refs), out_shape=(jax.Sh...]
    all_to_all x4 -> x0, waiting for transfers between devices: 24.2 us -> none  [the longest x1 12.9 us: local(): lax.all_to_all(stay_pieces, 'rep', split_axis=0, concat_axis=1, tiled=True)]
    all_to_all x2 -> x0, blocking collectives: 21.9 us -> none  [the longest x1 13.5 us: local(): lax.all_to_all(occupied.reshape(lists_here, owners, SLOT_L), 'owner', spl...]
    all_gather x1 -> x0, waiting for transfers between devices: 15.1 us -> none  [local(): lax.all_gather(refreshed_piece, 'rep', axis=0, tiled=True)]
    all_to_all x4 -> x0, starting transfers between devices: 13.4 us -> none  [the longest x1 3.52 us: local(): lax.all_to_all(stay_pieces, 'rep', split_axis=0, concat_axis=1, tiled=True)]
    all_gather x1 -> x0, blocking collectives: 5.07 us -> none  [local(): lax.all_gather(mass_piece, 'rep', axis=0, tiled=True)]
    unnamed x8 -> x12, local copies, waits for them, and re-layouts: 3.6 us -> 7.08 us
    all_to_all x9 -> x0, local copies, waits for them, and re-layouts: 2.94 us -> none  [the longest x1 1.08 us: local(): lax.all_to_all(stay_pieces, 'rep', split_axis=0, concat_axis=1, tiled=True)]
  transfers between devices with their start and end apart: 5 -> 0, of which waited for: 5 -> 0; matrix products, arithmetic and copies ran while one was open for 6% -> 0% of each run, Pallas kernels for 0% -> 0%
where the time goes in v1:
time: 46.1 us; the launch traced here: 45.9 us
  Pallas kernels  37.5 us (81%)
  local copies, waits for them, and re-layouts  7.75 us (17%)
  between operations  0.66 us (1%)
    pallas_call x1, Pallas kernels, fused(): pl.pallas_call(lambda *refs: fused_kernel(plan, *refs), out_shape=(jax.Sh...  37.5 us
    unnamed x12, local copies, waits for them, and re-layouts  7.08 us

profile of v1, /device:TPU:0, one launch (start us, length us, event | category | flops | bytes accessed | tf_op | source)
XLA Modules:
  0.0 45.9 jit_solution(2545637182679453716)
XLA Ops:
  0.6 0.7 %copy.8.refs_1_ = s32[8,1]{1,0:T(8,128)S(1)} copy(s32[8,1]{0,1:T(1,128)} %param.7) | data formatting | bytes 64 | tf_op args[1]
  1.4 0.0 copy-start
  1.4 1.6 %copy-done = bf16[8,128,1024]{2,1,0:T(8,128)(2,1)S(1)} copy-done((bf16[8,128,1024]{2,1,0:T(8,128)(2,1)S(1)}, bf16[8,128,1024]{2,1,0:T(8,128)(2,1)}, u32[]{:S(2)}) %copy-start) | copy-done | bytes 2097176
  3.0 0.0 copy-start.1
  3.0 1.2 %copy-done.1 = bf16[8,64,1024]{2,1,0:T(8,128)(2,1)S(1)} copy-done((bf16[8,64,1024]{2,1,0:T(8,128)(2,1)S(1)}, bf16[8,64,1024]{2,1,0:T(8,128)(2,1)}, u32[]{:S(2)}) %copy-start.1) | copy-done | bytes 1048600
  4.2 0.0 copy-start.2
  4.2 0.9 %copy-done.2 = bf16[64,1024]{1,0:T(8,128)(2,1)S(1)} copy-done((bf16[64,1024]{1,0:T(8,128)(2,1)S(1)}, bf16[64,1024]{1,0:T(8,128)(2,1)}, u32[]{:S(2)}) %copy-start.2) | copy-done | bytes 131096
  5.1 0.0 copy-start.3
  5.1 0.7 %copy-done.3 = s32[64]{0:T(128)S(1)} copy-done((s32[64]{0:T(128)S(1)}, s32[64]{0:T(128)}, u32[]{:S(2)}) %copy-start.3) | copy-done | bytes 280
  5.7 0.0 copy-start.4
  5.7 0.7 %copy-done.4 = f32[8]{0:T(128)S(1)} copy-done((f32[8]{0:T(128)S(1)}, f32[8]{0:T(128)}, u32[]{:S(2)}) %copy-start.4) | copy-done | bytes 56
  6.4 37.5 %shard_map.77 = (bf16[8,128,1024]{2,1,0:T(8,128)(2,1)S(1)}, f32[2,4,8,128]{3,2,1,0:T(8,128)S(1)}) custom-call(bf16[8,64,1024]{2,1,0:T(8,128)(2,1)S(1)} %copy-done.1, s32[8,1]{1,0:T(8,128)S(1)} %copy.8.refs_1_, bf16[64,1024]{1,0:T(8,128)(2,1)S(1)} %copy-done.2, s32[1,64]{1,0:T(1,128)S(1)} %bitcast.2, bf16[8,128,1024]{2,1,0:T(8,128)(2,1)S(1)} %copy-done, ...), custom_call_target="tpu_custom_call" | custom-call | tf_op jit(solution)/shard_map/pallas_call | solution.py:405
  43.9 0.7 %constant_dynamic-slice_fusion = f32[8,32]{1,0:T(8,128)} fusion(f32[8,128]{1,0:T(8,128)S(1)} %bitcast.3, s32[]{:T(128)S(6)} %select_n.3), kind=kLoop, calls=%fused_computation | loop fusion | bytes 2052 | tf_op jit(solution)/shard_map/dynamic_slice | solution.py:440
  44.6 1.3 %copy.10 = bf16[8,128,1024]{2,1,0:T(8,128)(2,1)} copy(bf16[8,128,1024]{2,1,0:T(8,128)(2,1)S(1)} %get-tuple-element.8) | data formatting | bytes 4194304
  (1 shorter events, 0.0 us)
Async XLA Ops:
  1.4 1.6 %copy-start = (bf16[8,128,1024]{2,1,0:T(8,128)(2,1)S(1)}, bf16[8,128,1024]{2,1,0:T(8,128)(2,1)}, u32[]{:S(2)}) copy-start(bf16[8,128,1024]{2,1,0:T(8,128)(2,1)} %refs_4_.1) | copy-start | bytes 6291460
  3.0 1.2 %copy-start.1 = (bf16[8,64,1024]{2,1,0:T(8,128)(2,1)S(1)}, bf16[8,64,1024]{2,1,0:T(8,128)(2,1)}, u32[]{:S(2)}) copy-start(bf16[8,64,1024]{2,1,0:T(8,128)(2,1)} %refs_0_.1) | copy-start | bytes 3145732
  4.2 0.9 %copy-start.2 = (bf16[64,1024]{1,0:T(8,128)(2,1)S(1)}, bf16[64,1024]{1,0:T(8,128)(2,1)}, u32[]{:S(2)}) copy-start(bf16[64,1024]{1,0:T(8,128)(2,1)} %refs_2_.1) | copy-start | bytes 393220
  5.1 0.7 %copy-start.3 = (s32[64]{0:T(128)S(1)}, s32[64]{0:T(128)}, u32[]{:S(2)}) copy-start(s32[64]{0:T(128)} %param.9) | copy-start | bytes 772
  5.7 0.7 %copy-start.4 = (f32[8]{0:T(128)S(1)}, f32[8]{0:T(128)}, u32[]{:S(2)}) copy-start(f32[8]{0:T(128)} %refs_5_.1) | copy-start | bytes 100
